TPU v7x, 128 devices: a whole 4x4x4 slice. The times are simulated.
128 devices in a mesh: ctx: 16 (over y, x), shard: 8 (over z, core).
Axes of the slice: x: 4, y: 4, z: 4, core: 2. Of those that a mesh axis runs over, the one named last changes fastest.
Arguments:
- queries: bfloat16 [4096, 12288], P('ctx', 'shard'), may hold values from -150 to 150
- latent_keys: bfloat16 [4096, 576], P('ctx'), may hold values from -8 to 8
- up_keys: bfloat16 [64, 128, 512], P('shard', 'ctx'), may hold values from -0.5 to 0.5
- up_values: bfloat16 [64, 512, 128], P('shard', 'ctx'), may hold values from -0.25 to 0.25
- out_weight: bfloat16 [64, 128, 7168], P('shard', None, 'ctx'), may hold values from -0.1875 to 0.1875
- keys_scale: int32 [64, 4], replicated, may hold values from -1 to 1
- values_scale: int32 [64, 4], replicated, may hold values from -1 to 1
- out_scale: int32 [64, 56], replicated, may hold values from -1 to 1
Outputs:
- mixed: bfloat16 [4096, 7168], P('ctx', 'shard')
All inputs are finite; a program needn't handle non-finite values.
Results may differ from a plain program's by a relative error of at most 0.019.
Values may be sent and summed in bfloat16 or wider, within the bound.
A program may use at most 192 MiB of HBM per device.

v0:
```python
import jax
import jax.numpy as jnp
from jax import lax
from jax.sharding import PartitionSpec as P

NOPE = 128
ROPE = 64
LATENT = 512
BLOCK = 128


def exponent_factor(exponents, block_size):
    return jnp.repeat(jnp.exp2(exponents.astype(jnp.float32)), block_size, axis=1)


def attend(status, rows, row_places, pieces, offset, latent_width, score_scale):
    key_places = jnp.arange(pieces.shape[0], dtype=jnp.int32)

    def update(current):
        running, totals, mixture = current
        scores = (
            lax.dot_general(
                rows, pieces, (((1,), (1,)), ((), ())), preferred_element_type=jnp.float32
            )
            * score_scale
        )
        visible = row_places[:, None] >= key_places[None, :]
        newest = jnp.maximum(running, jnp.max(jnp.where(visible, scores, -1e30), axis=1))
        weights = jnp.where(visible, jnp.exp(scores - newest[:, None]), 0.0)
        totals = jnp.sum(weights, axis=1)
        mixture = jnp.dot(
            weights.astype(jnp.bfloat16),
            pieces[:, :latent_width],
            preferred_element_type=jnp.float32,
        )
        return (newest, totals, mixture)

    def unchanged(current):
        return current

    return lax.cond(offset <= row_places[-1], update, unchanged, status)


def body(queries, latent_keys, up_keys, up_values, out_weight, keys_scale, values_scale, out_scale):
    tokens = queries.shape[0]
    head_count = up_keys.shape[0]
    halfway = tokens // 2
    ctx_place = lax.axis_index("ctx")
    shard_place = lax.axis_index("shard")
    head_first = shard_place * head_count
    key_tiles, value_tiles = (
        lax.all_gather(up_keys, "ctx", axis=1, tiled=True),
        lax.all_gather(up_values, "ctx", axis=1, tiled=True),
    )
    keys_factor = exponent_factor(
        lax.dynamic_slice_in_dim(keys_scale, head_first, head_count, 0), BLOCK
    )
    values_factor = exponent_factor(
        lax.dynamic_slice_in_dim(values_scale, head_first, head_count, 0), BLOCK
    )
    keys_weight = key_tiles * keys_factor[:, None, :].astype(jnp.bfloat16)
    values_weight = value_tiles * values_factor[:, :, None].astype(jnp.bfloat16)
    grouped = queries.reshape(tokens, head_count, NOPE + ROPE)
    leading = grouped[:halfway]
    second = grouped[halfway:]
    leading_begin = ctx_place * tokens
    second_begin = ctx_place * tokens + halfway

    def prepare(portion):
        latent_query = jnp.einsum(
            "thn,hnc->thc", portion[:, :, :NOPE], keys_weight, preferred_element_type=jnp.float32
        ).astype(jnp.bfloat16)
        joined = jnp.concatenate([latent_query, portion[:, :, NOPE:]], axis=2)
        return joined.reshape(halfway * head_count, LATENT + ROPE)

    def positions(begin_at):
        return begin_at + jnp.arange(halfway * head_count, dtype=jnp.int32) // head_count

    rows_leading = prepare(leading)
    rows_second = prepare(second)
    places_leading = positions(leading_begin)
    places_second = positions(second_begin)
    score_scale = (NOPE + ROPE) ** (-0.5)
    row_total = halfway * head_count
    initial = (
        jnp.full((row_total,), -1e30, jnp.float32),
        jnp.zeros((row_total,), jnp.float32),
        jnp.zeros((row_total, LATENT), jnp.float32),
    )
    pieces = lax.all_gather(latent_keys, "ctx", axis=0, tiled=True)
    offset = jnp.int32(0)

    def finish_half(status):
        totals = status[1]
        mixture = status[2]
        head_latent = (
            (mixture / totals[:, None]).astype(jnp.bfloat16).reshape(halfway, head_count, LATENT)
        )
        return jnp.einsum(
            "thc,hcv->thv", head_latent, values_weight, preferred_element_type=jnp.float32
        ).astype(jnp.bfloat16)

    value_leading = finish_half(
        attend(initial, rows_leading, places_leading, pieces, offset, LATENT, score_scale)
    )
    value_second = finish_half(
        attend(initial, rows_second, places_second, pieces, offset, LATENT, score_scale)
    )
    values = jnp.concatenate([value_leading, value_second], axis=0)
    out_factor = exponent_factor(
        lax.dynamic_slice_in_dim(out_scale, head_first, head_count, 0), BLOCK
    ).astype(jnp.bfloat16)
    scaled = lax.all_gather(out_weight, "ctx", axis=2, tiled=True) * out_factor[:, None, :]
    terms = jnp.einsum("thv,hvd->td", values, scaled, preferred_element_type=jnp.float32)
    return lax.psum_scatter(terms.astype(jnp.bfloat16), "shard", scatter_dimension=1, tiled=True)


def solution(mesh):
    return jax.shard_map(
        body,
        mesh=mesh,
        in_specs=(
            P("ctx", "shard"),
            P("ctx", None),
            P("shard", "ctx", None),
            P("shard", "ctx", None),
            P("shard", None, "ctx"),
            P(),
            P(),
            P(),
        ),
        out_specs=P("ctx", "shard"),
        check_vma=False,
    )
```

profile of v0, /device:TPU:30, one launch (start us, length us, event | category | flops | bytes accessed | tf_op | source)
XLA Modules:
  0.0 323.8 jit_solution(2758984416759772698)
XLA Ops:
  6.5 0.7 all-gather.7.cloned.1.call-update
  7.3 1.9 copy.42
  9.2 0.7 all-gather.5.cloned.1.call-update
  10.0 0.5 all-gather.11.cloned.1.call-update
  10.6 1.2 fusion.56
  12.0 0.6 slice.36
  13.6 0.6 slice.41
  15.2 0.8 exponential_convert_fusion.1
  16.0 0.8 exponential_convert_fusion.2
  17.0 35.6 %all-gather.7.cloned.1.call-done = bf16[8,128,512]{2,1,0:T(8,128)(2,1)} async-done(((bf16[8,8,512]{2,1,0:T(8,128)(2,1)}), bf16[8,128,512]{2,1,0:T(8,128)(2,1)}) %all-gather.7.cloned.1.call-update) | async-done | bytes 1048592 | tf_op jit(solution)/shard_map/all_gather | solution.py:52
  52.6 1.7 fusion.29
  54.3 1.1 pad_maximum_fusion
  55.5 1.7 fusion.30
  57.3 53.4 %all-gather.9.cloned.1.call-done = bf16[4096,576]{1,0:T(8,128)(2,1)} async-done(((bf16[256,576]{1,0:T(8,128)(2,1)}), bf16[4096,576]{1,0:T(8,128)(2,1)}) %all-gather.9.cloned.1.call-update) | async-done | bytes 4718608 | tf_op jit(solution)/shard_map/all_gather | solution.py:90
  110.7 23.5 %conditional.2 = (f32[1024]{0:T(1024)S(1)}, f32[1024,512]{1,0:T(8,128)S(1)}) conditional(s32[]{:T(128)} %bitcast.3, () %tuple.21, (s32[1024]{0:T(1024)S(1)}, s32[4096]{0:T(1024)S(1)}, bf16[128,8,576]{0,2,1:T(8,128)(2,1)}, bf16[4096,576]{1,0:T(8,128)(2,1)}) %tuple.22), branch_computations={%region_0.1_spmd, %region_1.4_spmd} | conditional | flops 9185524736 | bytes 64966672 | solution.py:41
  110.7 2.2 copy.43
  112.9 9.3 %fusion = (f32[1024]{0:T(1024)S(1)}, f32[1024,4096]{1,0:T(8,128)S(1)}) fusion(s32[4096]{0:T(1024)S(1)} %get-tuple-element.24, s32[1024]{0:T(1024)S(1)} %get-tuple-element.23, bf16[4096,576]{1,0:T(8,128)(2,1)} %get-tuple-element.26, bf16[128,8,576]{2,1,0:T(8,128)(2,1)S(1)} %copy.43), kind=kOutput, calls=%fused_computation.2 | convolution fusion | flops 4848614400 | bytes 22700032 | tf_op jit(solution)/shard_map/cond/branch_1_fun/dot_general | solution.py:22
  122.3 7.0 %fusion.3 = f32[1024,512]{1,0:T(8,128)S(1)} fusion(f32[1024,4096]{1,0:T(8,128)S(1)} %get-tuple-element.72, f32[1024]{0:T(1024)S(1)} %broadcast_maximum_fusion, s32[4096]{0:T(1024)S(1)} %get-tuple-element.24, s32[1024]{0:T(1024)S(1)} %get-tuple-element.23, bf16[4096,576]{1,0:T(8,128)(2,1)} %get-tuple-element.26), kind=kOutput, calls=%fused_computation.5 | convolution fusion | flops 4315938816 | bytes 23093248 | tf_op jit(solution)/shard_map/cond/branch_1_fun/dot_general | solution.py:31
  129.3 4.9 %fusion.2 = f32[1024]{0:T(1024)S(1)} fusion(f32[1024,4096]{1,0:T(8,128)S(1)} %get-tuple-element.72, f32[1024]{0:T(1024)S(1)} %broadcast_maximum_fusion, s32[4096]{0:T(1024)S(1)} %get-tuple-element.24, s32[1024]{0:T(1024)S(1)} %get-tuple-element.23), kind=kLoop, calls=%fused_computation.4 | loop fusion | flops 20970496 | bytes 16805888 | tf_op jit(solution)/shard_map/cond/branch_1_fun/reduce_sum | solution.py:30
  134.2 25.5 %conditional.3 = (f32[1024]{0:T(1024)S(1)}, f32[1024,512]{1,0:T(8,128)}) conditional(s32[]{:T(128)} %bitcast.9, () %tuple.23, (s32[1024]{0:T(1024)S(1)}, s32[4096]{0:T(1024)S(1)}, bf16[128,8,576]{0,2,1:T(8,128)(2,1)S(1)}, bf16[4096,576]{1,0:T(8,128)(2,1)}) %tuple.24), branch_computations={%region_4.5_spmd, %region_5.8_spmd} | conditional | flops 9185524736 | bytes 64966672 | solution.py:41
  134.5 2.0 copy.48
  136.5 9.7 %fusion.10 = (f32[1024]{0:T(1024)S(1)}, f32[1024,4096]{1,0:T(8,128)S(1)}) fusion(s32[4096]{0:T(1024)S(1)} %get-tuple-element.28, s32[1024]{0:T(1024)S(1)} %get-tuple-element.27, bf16[4096,576]{1,0:T(8,128)(2,1)} %get-tuple-element.30, bf16[128,8,576]{2,1,0:T(8,128)(2,1)} %copy.48), kind=kOutput, calls=%fused_computation.14 | convolution fusion | flops 4848614400 | bytes 22700032 | tf_op jit(solution)/shard_map/cond/branch_1_fun/dot_general | solution.py:22
  146.2 8.4 %fusion.13 = f32[1024,512]{1,0:T(8,128)} fusion(f32[1024,4096]{1,0:T(8,128)S(1)} %get-tuple-element.74, f32[1024]{0:T(1024)S(1)} %broadcast_maximum_fusion.1, s32[4096]{0:T(1024)S(1)} %get-tuple-element.28, s32[1024]{0:T(1024)S(1)} %get-tuple-element.27, bf16[4096,576]{1,0:T(8,128)(2,1)} %get-tuple-element.30), kind=kOutput, calls=%fused_computation.17 | convolution fusion | flops 4315938816 | bytes 23093248 | tf_op jit(solution)/shard_map/cond/branch_1_fun/dot_general | solution.py:31
  154.6 4.9 %fusion.12 = f32[1024]{0:T(1024)S(1)} fusion(f32[1024,4096]{1,0:T(8,128)S(1)} %get-tuple-element.74, f32[1024]{0:T(1024)S(1)} %broadcast_maximum_fusion.1, s32[4096]{0:T(1024)S(1)} %get-tuple-element.28, s32[1024]{0:T(1024)S(1)} %get-tuple-element.27), kind=kLoop, calls=%fused_computation.16 | loop fusion | flops 20970496 | bytes 16805888 | tf_op jit(solution)/shard_map/cond/branch_1_fun/reduce_sum | solution.py:30
  159.9 2.2 fusion.31
  162.2 1.8 fusion.36
  164.0 2.1 fusion.32
  166.2 91.5 %all-gather.11.cloned.1.call-done = bf16[8,128,7168]{1,2,0:T(8,128)(2,1)} async-done(((bf16[8,128,448]{1,2,0:T(8,128)(2,1)}), bf16[8,128,7168]{1,2,0:T(8,128)(2,1)}) %all-gather.11.cloned.1.call-update) | async-done | bytes 14680080 | tf_op jit(solution)/shard_map/all_gather | solution.py:113
  257.7 12.9 %fusion.25 = bf16[256,7168]{1,0:T(8,128)(2,1)} fusion(bf16[8,128,7168]{1,2,0:T(8,128)(2,1)} %all-gather.11.cloned.1.call-done, bf16[8,7168]{1,0:T(8,128)(2,1)S(1)} %broadcast_bitcast_fusion, bf16[128,8,128]{2,0,1:T(8,128)(2,1)S(1)} %fusion.32, bf16[128,8,128]{2,0,1:T(8,128)(2,1)S(1)} %fusion.31), kind=kOutput, calls=%fused_computation.27 | convolution fusion | flops 3768320000 | bytes 18989056 | tf_op jit(solution)/shard_map/thv,hvd->td/dot_general | solution.py:114
  270.6 5.9 %copy.56 = bf16[256,7168]{0,1:T(8,128)(2,1)} copy(bf16[256,7168]{1,0:T(8,128)(2,1)} %fusion.25) | data formatting | bytes 7340032
  276.5 38.8 %reduce-scatter.4.cloned.1.call-done = bf16[896,256]{1,0:T(8,128)(2,1)} async-done(((bf16[7168,256]{1,0:T(8,128)(2,1)}), bf16[896,256]{1,0:T(8,128)(2,1)}) %reduce-scatter.4.cloned.1.call-update) | async-done | bytes 458768
  315.3 2.0 copy.57
  (31 shorter events, 1.5 us)
Async XLA Ops:
  6.5 8.4 %copy-start = (s32[64,56]{0,1:T(8,128)S(1)}, s32[64,56]{0,1:T(8,128)}, u32[]{:S(2)}) copy-start(s32[64,56]{0,1:T(8,128)} %param.19) | copy-start | bytes 43012
  6.5 46.0 %all-gather.7.cloned.1.call-start = ((), (), s32[]{:S(2)}) async-start(), calls=%async_computation.2 | async-start | bytes 1114112 | tf_op jit(solution)/shard_map/all_gather | solution.py:52
  7.3 103.4 %all-gather.9.cloned.1.call-start = ((), (), s32[]{:S(2)}) async-start(), calls=%async_computation.3 | async-start | bytes 5570560 | tf_op jit(solution)/shard_map/all_gather | solution.py:90
  9.2 150.7 %all-gather.5.cloned.1.call-start = ((), (), s32[]{:S(2)}) async-start(), calls=%async_computation.1 | async-start | bytes 1114112 | tf_op jit(solution)/shard_map/all_gather | solution.py:53
  9.9 247.8 %all-gather.11.cloned.1.call-start = ((), (), s32[]{:S(2)}) async-start(), calls=%async_computation.4 | async-start | bytes 15597568 | tf_op jit(solution)/shard_map/all_gather | solution.py:113
  10.5 304.8 %reduce-scatter.4.cloned.1.call-start = ((), (), s32[]{:S(2)}) async-start(), calls=%async_computation.5 | async-start | bytes 4128768
  257.7 59.6 %copy-start.1 = (s32[64,56]{0,1:T(8,128)S(1)}, s32[64,56]{0,1:T(8,128)}, u32[]{:S(2)}) copy-start(s32[64,56]{0,1:T(8,128)} %param.19) | copy-start | bytes 43012
Sparse Core Ops, SparseCore 0:
  9.5 43.0 all-gather.6
  54.7 55.9 all-gather.8
  112.8 42.6 all-gather.4
  157.5 100.1 all-gather.10
  276.7 38.6 reduce-scatter.3
where the time goes:
time: 325 us; the launch traced here: 324 us
  waiting for transfers between devices  221 us (68%)
  matrix products  55.2 us (17%)
  local copies, waits for them, and re-layouts  17.4 us (5%)
  between operations  14.7 us (5%)
  other arithmetic  14.5 us (4%)
    all_gather x1, waiting for transfers between devices, body(): lax.all_gather(out_weight, 'ctx', axis=2, tiled=True)  91.5 us
    all_gather x1, waiting for transfers between devices, body(): pieces = lax.all_gather(latent_keys, 'ctx', axis=0, tiled=True)  53.4 us
    unnamed x6, waiting for transfers between devices  40.7 us
    all_gather x1, waiting for transfers between devices, body(): lax.all_gather(up_keys, 'ctx', axis=1, tiled=True)  35.6 us
    dot_general x2, matrix products, update(): lax.dot_general(rows, pieces, (((1,), (1,)), ((), ())), preferred_element...  19 us
    dot_general x2, matrix products, update(): jnp.dot(weights.astype(jnp.bfloat16), pieces[:, :latent_width], preferred...  15.4 us
    dot_general x1, matrix products, body(): jnp.einsum('thv,hvd->td', values, scaled, preferred_element_type=jnp.floa...  12.9 us
    unnamed x10, local copies, waits for them, and re-layouts  10.3 us
  transfers between devices with their start and end apart: 5, of which 4 were waited for; matrix products, arithmetic and copies ran while one was open for 20% of the time, Pallas kernels for 0%

commit v1 on v0

v1 whole, which is shorter than its diff:
```python
import functools

import jax
import jax.numpy as jnp
from jax import lax
from jax.experimental import pallas as pl
from jax.experimental.pallas import tpu as pltpu
from jax.sharding import PartitionSpec as P

NOPE = 128
ROPE = 64
HEAD = NOPE + ROPE
LATENT = 512
WIDE = LATENT + ROPE
VDIM = 128
HEADS = 8
TOKENS = 256
CHUNK = 4 * TOKENS
PAIR = 2 * TOKENS
COLS = 448
MESH = pl.DeviceIdType.MESH
FACTOR = (NOPE + ROPE) ** (-0.5) * 1.4426950408889634
F32 = jnp.float32
BF16 = jnp.bfloat16

PEERS = (
    [(0, d, 0, k) for d in (1, 2, 3) for k in (0, 1)]
    + [(d, 0, 0, k) for d in (1, 2, 3) for k in (0, 1)]
    + [(0, 0, d, 0) for d in (1, 2, 3)]
    + [(0, 0, 0, 1)]
)


def power(exponent):
    return jnp.where(exponent > 0, 2.0, jnp.where(exponent < 0, 0.5, 1.0)).astype(F32)


def lane_factor(values, width, shift):
    block = (lax.broadcasted_iota(jnp.int32, (1, width), 1) + shift) // 128
    result = jnp.full((1, width), values[0], F32)
    for k in range(1, len(values)):
        result = jnp.where(block == k, values[k], result)
    return result


def kernel(
    queries, latent_keys, up_keys, up_values, out_weight, keys_scale, values_scale, out_scale,
    out,
    kbuf, upk, upv, qbuf, acc, mx, ls, wbuf, wsend, abuf, cbuf, land1, land0, fin, outbuf,
    ssem, sw, sa, sas, sc, sl, rk1x, rk1y, rkz, rks, ru1, ru2, rv1, rv2, rwn, rwo, ra, ras, rl1, rl0, rf,
):
    ctx = lax.axis_index("ctx")
    shard = lax.axis_index("shard")
    y, x, z, c = ctx // 4, ctx % 4, shard // 2, shard % 2
    head_first = shard * HEADS

    def at(dy=0, dx=0, dz=0, dc=0):
        return (((y + dy) % 4) * 4 + (x + dx) % 4, ((z + dz) % 4) * 2 + (c + dc) % 2)

    pending = []
    counter = [0]

    def send(src, dst, recv, target):
        k = counter[0]
        counter[0] += 1
        copy = pltpu.make_async_remote_copy(
            src_ref=src, dst_ref=dst, send_sem=ssem.at[k], recv_sem=recv,
            device_id=target, device_id_type=MESH,
        )
        copy.start()
        pending.append((src, ssem.at[k]))

    def arrived(ref, sem):
        pltpu.make_async_copy(ref, ref, sem).wait()

    for half in range(2):
        rows = []
        for k in range(4):
            h = half * 4 + k
            f = lane_factor([power(keys_scale[head_first + h, b]) for b in range(4)], LATENT, 0)
            rows.append(up_keys[h].astype(F32) * f)
        upk[half, pl.ds(y, 1), pl.ds(x, 1)] = jnp.concatenate(rows, axis=0).astype(BF16)[None, None]
    for h in range(HEADS):
        f = power(values_scale[head_first + h, y])
        upv[pl.ds(y, 1), pl.ds(x, 1), h * 32 : (h + 1) * 32, :] = (
            (up_values[h].astype(F32) * f).astype(BF16)[None, None]
        )
    own_rows = pl.ds(shard * 32, 32)
    mine = pl.ds(shard * 128, 128)
    own_place = pl.ds(shard * 128 + x * 32, 32)

    barrier = pltpu.get_barrier_semaphore()
    for dy, dx, dz, dc in PEERS:
        pl.semaphore_signal(barrier, inc=1, device_id=at(dy, dx, dz, dc), device_id_type=MESH)
    pl.semaphore_wait(barrier, len(PEERS))

    for d in (1, 3, 2):
        send(latent_keys.at[own_rows], kbuf.at[y, own_place], rk1x, at(dx=d))
    pltpu.make_async_copy(latent_keys.at[own_rows], kbuf.at[y, own_place], rk1x).start()
    for d in (1, 3, 2):
        send(upk.at[:, y, x], upk.at[:, y, x], ru1.at[d], at(dy=d))

    def keys_along_z(i):
        j = (y + 4 - i) % 4
        for d in (1, 3, 2):
            send(kbuf.at[j, mine], kbuf.at[j, mine], rkz.at[i, d], at(dz=d))
        send(kbuf.at[j, mine], kbuf.at[j, mine], rks.at[i], at(dc=1))

    def keys_to_sibling(i):
        j = (y + 4 - i) % 4
        for d in (1, 3, 2):
            z_from = (z + 4 - d) % 4
            part = kbuf.at[j, pl.ds((z_from * 2 + c) * 128, 128)]
            arrived(part, rkz.at[i, d])
            send(part, part, rks.at[i], at(dc=1))

    def keys_ready(i):
        arrived(kbuf.at[(y + 4 - i) % 4, pl.ds(0, 512)], rks.at[i])

    arrived(kbuf.at[y, mine], rk1x)
    keys_along_z(0)
    for d in (1, 2, 3):
        send(kbuf.at[y, mine], kbuf.at[y, mine], rk1y.at[d], at(dy=d))
    for d in (1, 2, 3):
        arrived(upk.at[:, (y + 4 - d) % 4, x], ru1.at[d])
    for half in range(2):
        for d in (1, 3, 2):
            send(upk.at[half, :, x], upk.at[half, :, x], ru2.at[half, d], at(dx=d))
    for d in (1, 3, 2):
        send(upv.at[y, x], upv.at[y, x], rv1.at[d], at(dy=d))

    first_block = (ctx * 7) // 2
    shift = (ctx % 2) * 64
    for h in range(HEADS):
        f = lane_factor(
            [power(out_scale[head_first + h, first_block + b]) for b in range(4)], COLS, shift
        )
        wsend[h * VDIM : (h + 1) * VDIM, :] = (out_weight[h].astype(F32) * f).astype(BF16)
    owner = y // 2
    up_one, down_one = (((y + 1) % 4) * 4 + x, z * 2 + owner), (((y + 3) % 4) * 4 + x, z * 2 + owner)
    for order in range(2):
        part_up, part_down = pl.ds(order * 512, 512), pl.ds((1 - order) * 512, 512)
        send(wsend.at[part_up], wbuf.at[y % 2, c, part_up], rwn.at[c, order], up_one)
        send(wsend.at[part_down], wbuf.at[y % 2, c, part_down], rwn.at[c, 1 - order], down_one)
    own_weight = owner == c

    @pl.when(own_weight)
    def _():
        pltpu.make_async_copy(wsend, wbuf.at[y % 2, c], rwo.at[c]).start()

    sibling_weight = pltpu.make_async_remote_copy(
        src_ref=wsend, dst_ref=wbuf.at[y % 2, c], send_sem=sw.at[0], recv_sem=rwo.at[c],
        device_id=at(dc=1), device_id_type=MESH,
    )

    @pl.when(jnp.logical_not(own_weight))
    def _():
        sibling_weight.start()

    near_slot = (y + 1) % 2
    from_below = (2 * c + near_slot + 4 - y) % 4 == 3

    def weight_relay():
        half = jnp.where(from_below, 0, 1)
        for k in range(2):
            arrived(wbuf.at[near_slot, k, pl.ds(0, 512)], rwn.at[k, half])
        part = wbuf.at[near_slot, :, pl.ds(half * 512, 512)]
        step = jnp.where(from_below, 1, 3)
        send(part, part, rwo.at[half], (((y + step) % 4) * 4 + x, shard))

    def weight_ready():
        rest = jnp.where(from_below, 1, 0)
        for k in range(2):
            arrived(wbuf.at[near_slot, k, pl.ds(0, 512)], rwn.at[k, rest])
        for k in range(2):
            arrived(wbuf.at[y % 2, k], rwo.at[k])

    def make_queries(half):
        for d in (1, 2, 3):
            arrived(upk.at[half, :, (x + 4 - d) % 4], ru2.at[half, d])
        tiles = upk[half].astype(F32).reshape(16, 4, 8, LATENT)
        for k in range(4):
            h = half * 4 + k
            weight = tiles[:, k].reshape(NOPE, LATENT).astype(BF16)
            content = queries[:, h * HEAD : h * HEAD + NOPE]
            latent = jnp.dot(content, weight, preferred_element_type=F32).astype(BF16)
            qbuf[h * TOKENS : (h + 1) * TOKENS, :LATENT] = latent
            qbuf[h * TOKENS : (h + 1) * TOKENS, LATENT:] = queries[:, h * HEAD + NOPE : (h + 1) * HEAD]

    def update(pair, i):
        rows = pl.ds(pair * PAIR, PAIR)
        j = (y + 4 - i) % 4
        scores = lax.dot_general(
            qbuf[rows, :], kbuf[j], (((1,), (1,)), ((), ())), preferred_element_type=F32
        )
        latent = kbuf[j, :, :LATENT]
        if i == 0:
            row = lax.broadcasted_iota(jnp.int32, (PAIR, CHUNK), 0) % TOKENS + x * TOKENS
            col = lax.broadcasted_iota(jnp.int32, (PAIR, CHUNK), 1)
            place = ((col % 128) // 32) * TOKENS + (col // 128) * 32 + col % 32
            scores = jnp.where(place <= row, scores, -1e30)
            newest = jnp.max(scores, axis=1, keepdims=True)
            weights = jnp.exp2((scores - newest) * FACTOR)
            ls[rows, :] = jnp.broadcast_to(jnp.sum(weights, axis=1, keepdims=True), (PAIR, 128))
            acc[rows, :] = jnp.dot(weights.astype(BF16), latent, preferred_element_type=F32)
        else:
            last = mx[rows, :1]
            newest = jnp.maximum(last, jnp.max(scores, axis=1, keepdims=True))
            weights = jnp.exp2((scores - newest) * FACTOR)
            decay = jnp.exp2((last - newest) * FACTOR)
            ls[rows, :] = ls[rows, :] * decay + jnp.sum(weights, axis=1, keepdims=True)
            acc[rows, :] = acc[rows, :] * decay + jnp.dot(
                weights.astype(BF16), latent, preferred_element_type=F32
            )
        mx[rows, :] = jnp.broadcast_to(newest, (PAIR, 128))

    def pair_lanes(pair, core):
        return pl.ds(pl.multiple_of(core * 1024 + pair * 256, 256), 256)

    def finish(pair):
        for k in range(2):
            h = pair * 2 + k
            rows = pl.ds(h * TOKENS, TOKENS)
            head_latent = (acc[rows, :] / ls[rows, :1]).astype(BF16)
            tile = upv[:, :, h * 32 : (h + 1) * 32, :].reshape(LATENT, VDIM)
            value = jnp.dot(head_latent, tile, preferred_element_type=F32).astype(BF16)
            lanes = pl.ds(pl.multiple_of(c * 1024 + h * VDIM, VDIM), VDIM)
            abuf[pl.ds(x, 1), :, lanes] = value[None]
        part = abuf.at[x, :, pair_lanes(pair, c)]
        for d in (1, 3, 2):
            send(part, part, ra.at[pair, d], at(dx=d))

    def values_to_sibling(pair):
        for d in (1, 2, 3):
            arrived(abuf.at[(x + 4 - d) % 4, :, pair_lanes(pair, c)], ra.at[pair, d])
        part = abuf.at[:, :, pair_lanes(pair, c)]
        send(part, part, ras.at[pair], at(dc=1))

    def values_ready(pair):
        arrived(abuf.at[:, :, pair_lanes(pair, 1 - c)], ras.at[pair])

    make_queries(0)
    keys_to_sibling(0)
    for d in (1, 2, 3):
        arrived(upv.at[(y + 4 - d) % 4, x], rv1.at[d])
    for d in (1, 3, 2):
        send(upv.at[:, x], upv.at[:, x], rv2.at[d], at(dx=d))
    keys_ready(0)
    for i in range(4):
        if i < 3:
            arrived(kbuf.at[(y + 3 - i) % 4, mine], rk1y.at[i + 1])
            keys_along_z(i + 1)
        if i == 2:
            weight_relay()
        for pair in range(2):
            if i == 0:
                update(pair, i)
            else:
                pl.when(y >= i)(functools.partial(update, pair, i))
            if pair == 0 and i < 3:
                keys_to_sibling(i + 1)
        if i < 3:
            keys_ready(i + 1)
    make_queries(1)
    for d in (1, 2, 3):
        arrived(upv.at[:, (x + 4 - d) % 4], rv2.at[d])
    finish(0)
    finish(1)
    for pair in range(2, 4):
        for i in range(4):
            if i == 0:
                update(pair, i)
            else:
                pl.when(y >= i)(functools.partial(update, pair, i))
        values_to_sibling(pair - 2)
        finish(pair)
    values_to_sibling(2)
    values_to_sibling(3)
    weight_ready()
    for pair in range(4):
        values_ready(pair)

    near = (z + 1) % 2
    other = z % 2
    is_own = z // 2 == c
    near_up = (2 * c + near + 4 - z) % 4 == 1
    near_half = jnp.where(near_up, 0, 1)
    z_near = jnp.where(near_up, 1, 3)

    def project(slot, t):
        part = jnp.dot(abuf[t, :, :1024], wbuf[slot, 0], preferred_element_type=F32)
        part += jnp.dot(abuf[t, :, 1024:], wbuf[slot, 1], preferred_element_type=F32)
        cbuf[slot, t] = part.astype(BF16)

    def far_copy(t, half):
        return pltpu.make_async_remote_copy(
            src_ref=cbuf.at[other, t, pl.ds(half * 128, 128)], dst_ref=land1.at[t],
            send_sem=sc.at[t, half], recv_sem=rl1.at[t],
            device_id=at(dz=1 if half == 0 else 3), device_id_type=MESH,
        )

    def near_copy(t):
        return pltpu.make_async_remote_copy(
            src_ref=cbuf.at[near, t], dst_ref=land0.at[near_half, t],
            send_sem=sl.at[t], recv_sem=rl0.at[near_half, t],
            device_id=at(dz=z_near), device_id_type=MESH,
        )

    first = jnp.where(is_own, near, other)

    def first_step(t, carry):
        project(first, t)

        @pl.when(jnp.logical_not(is_own))
        def _():
            far_copy(t, 0).start()
            far_copy(t, 1).start()

        return carry

    def second_step(t, carry):
        project(1 - first, t)
        return carry

    def near_step(t, carry):
        arrived(land1.at[t], rl1.at[t])
        rows = pl.ds(near_half * 128, 128)
        total = cbuf[near, t, rows].astype(F32) + land1[t].astype(F32)
        cbuf[near, t, rows] = total.astype(BF16)
        near_copy(t).start()
        return carry

    lax.fori_loop(0, 4, first_step, 0)
    lax.fori_loop(0, 4, second_step, 0)
    lax.fori_loop(0, 4, near_step, 0)

    receiver = x // 2

    def final_copy(t):
        return pltpu.make_async_remote_copy(
            src_ref=fin.at[t], dst_ref=outbuf.at[x % 2], send_sem=sa.at[t], recv_sem=rf.at[x % 2],
            device_id=(y * 4 + t, z * 2 + receiver), device_id_type=MESH,
        )

    def local_copy(t):
        return pltpu.make_async_copy(fin.at[t], outbuf.at[x % 2], rf.at[x % 2])

    def final_step(t, carry):
        arrived(land0.at[0, t], rl0.at[0, t])
        arrived(land0.at[1, t], rl0.at[1, t])
        total = cbuf[other, t].astype(F32) + land0[0, t].astype(F32) + land0[1, t].astype(F32)
        fin[t] = total.astype(BF16)
        here = jnp.logical_and(t == x, receiver == c)

        @pl.when(here)
        def _():
            local_copy(t).start()

        @pl.when(jnp.logical_not(here))
        def _():
            final_copy(t).start()

        return carry

    @pl.when(is_own)
    def _():
        lax.fori_loop(0, 4, final_step, 0)

    for k in range(2):
        arrived(outbuf.at[k], rf.at[k])
    out[:, :COLS] = outbuf[0]
    out[:, COLS:] = outbuf[1]

    for ref, sem in pending:
        arrived(ref, sem)

    @pl.when(jnp.logical_not(own_weight))
    def _():
        sibling_weight.wait_send()

    def sent_near(t, carry):
        near_copy(t).wait_send()
        return carry

    def sent_far(t, carry):
        far_copy(t, 0).wait_send()
        far_copy(t, 1).wait_send()
        return carry

    def sent_final(t, carry):
        @pl.when(jnp.logical_not(jnp.logical_and(t == x, receiver == c)))
        def _():
            final_copy(t).wait_send()

        return carry

    lax.fori_loop(0, 4, sent_near, 0)

    @pl.when(jnp.logical_not(is_own))
    def _():
        lax.fori_loop(0, 4, sent_far, 0)

    @pl.when(is_own)
    def _():
        lax.fori_loop(0, 4, sent_final, 0)


def body(queries, latent_keys, up_keys, up_values, out_weight, keys_scale, values_scale, out_scale):
    vmem = pl.BlockSpec(memory_space=pltpu.VMEM)
    smem = pl.BlockSpec(memory_space=pltpu.SMEM)
    dma = pltpu.SemaphoreType.DMA
    return pl.pallas_call(
        kernel,
        out_shape=jax.ShapeDtypeStruct((TOKENS, 2 * COLS), BF16),
        in_specs=[vmem] * 5 + [smem] * 3,
        out_specs=vmem,
        scratch_shapes=[
            pltpu.VMEM((4, CHUNK, WIDE), BF16),
            pltpu.VMEM((2, 4, 4, 32, LATENT), BF16),
            pltpu.VMEM((4, 4, 256, VDIM), BF16),
            pltpu.VMEM((HEADS * TOKENS, WIDE), BF16),
            pltpu.VMEM((HEADS * TOKENS, LATENT), F32),
            pltpu.VMEM((HEADS * TOKENS, 128), F32),
            pltpu.VMEM((HEADS * TOKENS, 128), F32),
            pltpu.VMEM((2, 2, 1024, COLS), BF16),
            pltpu.VMEM((1024, COLS), BF16),
            pltpu.VMEM((4, TOKENS, 2048), BF16),
            pltpu.VMEM((2, 4, TOKENS, COLS), BF16),
            pltpu.VMEM((4, 128, COLS), BF16),
            pltpu.VMEM((2, 4, TOKENS, COLS), BF16),
            pltpu.VMEM((4, TOKENS, COLS), BF16),
            pltpu.VMEM((2, TOKENS, COLS), BF16),
            dma((96,)),
            dma((1,)),
            dma((4,)),
            dma((4,)),
            dma((4, 2)),
            dma((4,)),
            dma,
            dma((4,)),
            dma((4, 4)),
            dma((4,)),
            dma((4,)),
            dma((2, 4)),
            dma((4,)),
            dma((4,)),
            dma((2, 2)),
            dma((2,)),
            dma((4, 4)),
            dma((4,)),
            dma((4,)),
            dma((2, 4)),
            dma((2,)),
        ],
        compiler_params=pltpu.CompilerParams(
            collective_id=0, has_side_effects=True, vmem_limit_bytes=56 * 2**20
        ),
        name="attention",
    )(queries, latent_keys, up_keys, up_values, out_weight, keys_scale, values_scale, out_scale)


def solution(mesh):
    return jax.shard_map(
        body,
        mesh=mesh,
        in_specs=(
            P("ctx", "shard"),
            P("ctx", None),
            P("shard", "ctx", None),
            P("shard", "ctx", None),
            P("shard", None, "ctx"),
            P(),
            P(),
            P(),
        ),
        out_specs=P("ctx", "shard"),
        check_vma=False,
    )
```

time: 325 us -> 130 us (0.40)
  waiting for transfers between devices: 221 us -> 0 us
  Pallas kernels: 0 us -> 121 us
  matrix products: 55.2 us -> 0 us
  between operations: 14.7 us -> 0.01 us
  other arithmetic: 14.5 us -> 0 us
  local copies, waits for them, and re-layouts: 17.4 us -> 8.69 us
    all_gather x4 -> x0, waiting for transfers between devices: 181 us -> none  [the longest x1 91.5 us: body(): lax.all_gather(out_weight, 'ctx', axis=2, tiled=True)]
    pallas_call x0 -> x1, Pallas kernels: none -> 121 us  [body(): pl.pallas_call(kernel, out_shape=jax.ShapeDtypeStruct((TOKENS, 2 * COLS),...]
    dot_general x9 -> x0, matrix products: 55.2 us -> none  [the longest x2 19 us: update(): lax.dot_general(rows, pieces, (((1,), (1,)), ((), ())), preferred_element...]
    unnamed x6 -> x0, waiting for transfers between devices: 40.7 us -> none
    reduce_sum x2 -> x0, other arithmetic: 9.75 us -> none  [update(): totals = jnp.sum(weights, axis=1)]
    another operation x2 -> x0, local copies, waits for them, and re-layouts: 4.23 us -> none
  transfers between devices with their start and end apart: 5 -> 0, of which waited for: 4 -> 0; matrix products, arithmetic and copies ran while one was open for 20% -> 0% of each run, Pallas kernels for 0% -> 0%
where the time goes in v1:
time: 130 us
  Pallas kernels  121 us (93%)
  local copies, waits for them, and re-layouts  8.69 us (7%)
    pallas_call x1, Pallas kernels, body(): pl.pallas_call(kernel, out_shape=jax.ShapeDtypeStruct((TOKENS, 2 * COLS),...  121 us
    unnamed x10, local copies, waits for them, and re-layouts  8.69 us

profile of v1, /device:TPU:30, one launch (start us, length us, event | category | flops | bytes accessed | tf_op | source)
XLA Modules:
  0.0 129.6 jit_solution(17788846936440556749)
XLA Ops:
  0.0 0.0 copy-start
  0.0 0.0 copy-start.1
  0.0 1.4 %copy.11.keys_scale = s32[64,4]{1,0:T(8,128)} copy(s32[64,4]{0,1:T(4,128)} %param.13) | data formatting | bytes 2048 | tf_op args[5]
  1.4 0.0 copy-done.1
  1.4 0.7 copy.12.values_scale
  2.1 0.0 copy-done
  2.1 0.7 copy.13.out_scale
  2.8 1.9 %copy.9.latent_keys = bf16[256,576]{1,0:T(8,128)(2,1)} copy(bf16[256,576]{0,1:T(8,128)(2,1)} %param.9) | data formatting | bytes 589824 | tf_op args[1]
  4.6 2.2 %copy.10.out_weight = bf16[8,128,448]{2,1,0:T(8,128)(2,1)} copy(bf16[8,128,448]{1,2,0:T(8,128)(2,1)} %param.12) | data formatting | bytes 1835008 | tf_op args[4]
  6.9 120.9 %attention.1 = bf16[256,896]{1,0:T(8,128)(2,1)} custom-call(bf16[256,1536]{1,0:T(8,128)(2,1)} %queries.1, bf16[256,576]{1,0:T(8,128)(2,1)} %copy.9.latent_keys, bf16[8,8,512]{2,1,0:T(8,128)(2,1)} %up_keys.1, bf16[8,32,128]{2,1,0:T(8,128)(2,1)} %up_values.1, bf16[8,128,448]{2,1,0:T(8,128)(2,1)} %copy.10.out_weight, s32[64,4]{1,0:T(8,128)} %copy.11.keys_scale, ...), custom_call_target="tpu_custom_call" | custom-call | tf_op jit(solution)/shard_map/attention/pallas_call | solution.py:412
  127.7 1.8 %copy.15 = bf16[256,896]{1,0:T(8,128)(2,1)} copy(bf16[256,896]{1,0:T(8,128)(2,1)} %attention.1) | data formatting | bytes 917504
Async XLA Ops:
  0.0 2.1 %copy-start = (s32[64,56]{0,1:T(8,128)S(1)}, s32[64,56]{0,1:T(8,128)}, u32[]{:S(2)}) copy-start(s32[64,56]{0,1:T(8,128)} %param.15) | copy-start | bytes 43012
  0.0 1.4 %copy-start.1 = (s32[64,4]{0,1:T(4,128)S(1)}, s32[64,4]{0,1:T(4,128)}, u32[]{:S(2)}) copy-start(s32[64,4]{0,1:T(4,128)} %param.14) | copy-start | bytes 3076

commit v2 on v1

v2 whole, which is shorter than its diff:
```python
import functools

import jax
import jax.numpy as jnp
from jax import lax
from jax.experimental import pallas as pl
from jax.experimental.pallas import tpu as pltpu
from jax.sharding import PartitionSpec as P

NOPE = 128
ROPE = 64
HEAD = NOPE + ROPE
LATENT = 512
WIDE = LATENT + ROPE
VDIM = 128
HEADS = 8
TOKENS = 256
CHUNK = 4 * TOKENS
COLS = 448
PIECE = WIDE // 4
MESH = pl.DeviceIdType.MESH
FACTOR = (NOPE + ROPE) ** (-0.5) * 1.4426950408889634
F32 = jnp.float32
BF16 = jnp.bfloat16

PEERS = (
    [(0, d, 0, k) for d in (1, 2, 3) for k in (0, 1)]
    + [(d, 0, 0, k) for d in (1, 2, 3) for k in (0, 1)]
    + [(0, 0, d, 0) for d in (1, 2, 3)]
    + [(0, 0, 0, 1)]
)


def power(exponent):
    return jnp.where(exponent > 0, 2.0, jnp.where(exponent < 0, 0.5, 1.0)).astype(F32)


def block_factor(values, shape, dim, shift):
    block = (lax.broadcasted_iota(jnp.int32, shape, dim) + shift) // 128
    result = jnp.full(shape, values[0], F32)
    for k in range(1, len(values)):
        result = jnp.where(block == k, values[k], result)
    return result


def kernel(
    queries, latent_keys, up_keys, up_values, out_weight, keys_scale, values_scale, out_scale,
    out,
    kbuf, upk, upv, qbuf, acc, mx, ls, wbuf, wsend, abuf, cbuf, land1, land0, fin, outbuf,
    ssem, sw, sa, sc, sl, rk1x, rk1y, rkz, rks, ru1, ru2, rv1, rv2, rwn, rwo, ra, ras, rl1, rl0, rf,
):
    ctx = lax.axis_index("ctx")
    shard = lax.axis_index("shard")
    y, x, z, c = ctx // 4, ctx % 4, shard // 2, shard % 2
    head_first = shard * HEADS

    def at(dy=0, dx=0, dz=0, dc=0):
        return (((y + dy) % 4) * 4 + (x + dx) % 4, ((z + dz) % 4) * 2 + (c + dc) % 2)

    barrier = pltpu.get_barrier_semaphore()
    for dy, dx, dz, dc in PEERS:
        pl.semaphore_signal(barrier, inc=1, device_id=at(dy, dx, dz, dc), device_id_type=MESH)

    pending = []
    counter = [0]

    def send(src, dst, recv, target, condition=None):
        k = counter[0]
        counter[0] += 1
        copy = pltpu.make_async_remote_copy(
            src_ref=src, dst_ref=dst, send_sem=ssem.at[k], recv_sem=recv,
            device_id=target, device_id_type=MESH,
        )
        copy.start()
        pending.append((src, k, condition))

    def arrived(ref, sem):
        pltpu.make_async_copy(ref, ref, sem).wait()

    for half in range(2):
        rows = []
        for k in range(4):
            h = half * 4 + k
            f = block_factor(
                [power(keys_scale[b, head_first + h]) for b in range(4)], (1, LATENT), 1, 0
            )
            rows.append(up_keys[h].astype(F32) * f)
        upk[half, pl.ds(y, 1), pl.ds(x, 1)] = jnp.concatenate(rows, axis=0).astype(BF16)[None, None]

    for h in range(HEADS):
        f = power(values_scale[y, head_first + h])
        upv[pl.ds(y, 1), pl.ds(x, 1), h * 32 : (h + 1) * 32, :] = (
            (up_values[h].astype(F32) * f).astype(BF16)[None, None]
        )

    chunk = [(y + 4 - i) % 4 for i in range(4)]
    features = [pl.ds(((z + d) % 4) * PIECE, PIECE) for d in range(4)]
    my_lanes = pl.ds(pl.multiple_of(c * 512, 512), 512)
    my_halves = [pl.ds(pl.multiple_of(c * 512 + k * 256, 256), 256) for k in range(2)]
    its_lanes = pl.ds(pl.multiple_of((1 - c) * 512, 512), 512)
    own_lanes = pl.ds(pl.multiple_of(c * 128, 128), 128)
    own_place = pl.ds(pl.multiple_of(c * 512 + x * 128, 128), 128)

    pl.semaphore_wait(barrier, len(PEERS))

    own_keys, own_slot = latent_keys.at[features[0], own_lanes], kbuf.at[y, features[0], own_place]
    for d in (1, 3, 2):
        send(own_keys, own_slot, rk1x, at(dx=d))
    pltpu.make_async_copy(own_keys, own_slot, rk1x).start()
    for d in (1, 3, 2):
        piece = upk.at[0, y, x]
        send(piece, piece, ru1.at[0, d], at(dy=d))

    def needed(i, action):
        if i == 0:
            action()
        else:
            pl.when(y >= i)(action)

    def keys_along_z(i):
        part = kbuf.at[chunk[i], features[0], my_lanes]
        condition = None if i == 0 else y >= i

        def action():
            if i > 0:
                arrived(part, rk1y.at[i])
            for d in (1, 3):
                send(part, part, rkz.at[i, d], at(dz=d), condition)
            send(part, part, rks.at[i], at(dc=1), condition)

        needed(i, action)

    def keys_relay(i):
        condition = None if i == 0 else y >= i

        def action():
            for d in (1, 3):
                part = kbuf.at[chunk[i], features[4 - d], my_lanes]
                arrived(part, rkz.at[i, d])
                half = kbuf.at[chunk[i], features[4 - d], my_halves[d // 2]]
                send(half, half, rkz.at[i, 2], at(dz=d), condition)
                send(part, part, rks.at[i], at(dc=1), condition)

        needed(i, action)

    def keys_far(i):
        condition = None if i == 0 else y >= i

        def action():
            part = kbuf.at[chunk[i], features[2], my_lanes]
            arrived(part, rkz.at[i, 2])
            send(part, part, rks.at[i], at(dc=1), condition)

        needed(i, action)

    def keys_ready(i):
        needed(i, lambda: arrived(kbuf.at[chunk[i], :, its_lanes], rks.at[i]))

    first_block = (ctx * 7) // 2
    shift = (ctx % 2) * 64
    for h in range(HEADS):
        f = block_factor(
            [power(out_scale[first_block + b, head_first + h]) for b in range(4)], (COLS, 1), 0, shift
        )
        wsend[:, h * VDIM : (h + 1) * VDIM] = (out_weight[h].astype(F32) * f).astype(BF16)

    arrived(kbuf.at[y, features[0], my_lanes], rk1x)
    keys_along_z(0)
    for d in (1, 2, 3):
        part = kbuf.at[y, features[0], my_lanes]
        condition = y + d < 4
        pl.when(condition)(lambda: send(part, part, rk1y.at[d], at(dy=d), condition))
    y_from = [(y + 4 - d) % 4 for d in range(4)]
    x_from = [(x + 4 - d) % 4 for d in range(4)]
    for d in (1, 3, 2):
        arrived(upk.at[0, y_from[d], x], ru1.at[0, d])
    for d in (1, 3, 2):
        send(upk.at[0, :, x], upk.at[0, :, x], ru2.at[0, d], at(dx=d))
    for d in (1, 3, 2):
        send(upk.at[1, y, x], upk.at[1, y, x], ru1.at[1, d], at(dy=d))
    for d in (1, 3, 2):
        send(upv.at[y, x], upv.at[y, x], rv1.at[d], at(dy=d))
    keys_relay(0)
    keys_along_z(1)
    for d in (1, 3, 2):
        arrived(upk.at[0, :, x_from[d]], ru2.at[0, d])

    owner = y // 2
    up_one, down_one = (((y + 1) % 4) * 4 + x, z * 2 + owner), (((y + 3) % 4) * 4 + x, z * 2 + owner)
    weight_lanes = pl.ds(pl.multiple_of(c * 1024, 1024), 1024)
    weight_rows = [pl.ds(0, COLS // 2), pl.ds(COLS // 2, COLS // 2)]
    for order in range(2):
        for half, target in ((order, up_one), (1 - order, down_one)):
            rows = weight_rows[half]
            send(wsend.at[rows], wbuf.at[y % 2, rows, weight_lanes], rwn.at[c, half], target)
    own_weight = owner == c

    @pl.when(own_weight)
    def _():
        pltpu.make_async_copy(wsend, wbuf.at[y % 2, :, weight_lanes], rwo.at[c]).start()

    sibling_weight = pltpu.make_async_remote_copy(
        src_ref=wsend, dst_ref=wbuf.at[y % 2, :, weight_lanes], send_sem=sw.at[0], recv_sem=rwo.at[c],
        device_id=at(dc=1), device_id_type=MESH,
    )

    @pl.when(jnp.logical_not(own_weight))
    def _():
        sibling_weight.start()

    near_slot = (y + 1) % 2
    from_below = (2 * c + near_slot + 4 - y) % 4 == 3

    def weight_relay():
        half = jnp.where(from_below, 0, 1)
        for k in range(2):
            arrived(wbuf.at[near_slot, weight_rows[0], pl.ds(0, 1024)], rwn.at[k, half])
        part = wbuf.at[near_slot, pl.ds(half * (COLS // 2), COLS // 2)]
        step = jnp.where(from_below, 1, 3)
        send(part, part, rwo.at[half], (((y + step) % 4) * 4 + x, shard))

    def weight_ready():
        rest = jnp.where(from_below, 1, 0)
        for k in range(2):
            arrived(wbuf.at[near_slot, weight_rows[0], pl.ds(0, 1024)], rwn.at[k, rest])
        for k in range(2):
            arrived(wbuf.at[y % 2, :, pl.ds(0, 1024)], rwo.at[k])

    def make_queries(half):
        tiles = upk[half].astype(F32).reshape(16, 4, 8, LATENT)
        for k in range(4):
            h = half * 4 + k
            weight = tiles[:, k].reshape(NOPE, LATENT).astype(BF16)
            content = queries[:, h * HEAD : h * HEAD + NOPE]
            latent = jnp.dot(content, weight, preferred_element_type=F32).astype(BF16)
            rotary = queries[:, h * HEAD + NOPE : (h + 1) * HEAD]
            for part in range(2):
                rows = slice(part * 1024 + h * 128, part * 1024 + (h + 1) * 128)
                tokens = slice(part * 128, (part + 1) * 128)
                qbuf[rows, :LATENT] = latent[tokens]
                qbuf[rows, LATENT:] = rotary[tokens]

    def chunk_of(i):
        return (y + 4 - i) % 4

    def attend(units, first=False):

        def score(i, part, group):
            first_row = part * 1024 + group * 512
            scores = jnp.dot(
                qbuf[first_row : first_row + 512, :], kbuf[chunk_of(i)], preferred_element_type=F32
            )
            if first:
                row = lax.broadcasted_iota(jnp.int32, (512, CHUNK), 0) % 128 + (x * TOKENS + part * 128)
                col = lax.broadcasted_iota(jnp.int32, (512, CHUNK), 1)
                place = ((col % 512) // 128) * TOKENS + (col // 512) * 128 + col % 128
                scores = jnp.where(place <= row, scores, -1e30)
            return scores

        def mix(scores, i, part, group):
            rows = slice(part * 1024 + group * 512, part * 1024 + group * 512 + 512)
            newest = jnp.max(scores, axis=1, keepdims=True)
            if not first:
                last = mx[rows, :1]
                newest = jnp.maximum(last, newest)
            weights = jnp.exp2((scores - newest) * FACTOR)
            total = jnp.sum(weights, axis=1, keepdims=True)
            mx[rows, :] = jnp.broadcast_to(newest, (512, 128))
            mixture = lax.dot_general(
                weights.astype(BF16), kbuf[chunk_of(i), :LATENT], (((1,), (1,)), ((), ())),
                preferred_element_type=F32,
            )
            if first:
                ls[rows, :] = jnp.broadcast_to(total, (512, 128))
                acc[rows, :] = mixture
            else:
                decay = jnp.exp2((last - newest) * FACTOR)
                ls[rows, :] = ls[rows, :] * decay + total
                acc[rows, :] = acc[rows, :] * decay + mixture

        scores = score(*units[0])
        for n, unit in enumerate(units):
            following = score(*units[n + 1]) if n + 1 < len(units) else None
            mix(scores, *unit)
            scores = following

    def value_lanes(core):
        return pl.ds(pl.multiple_of(core * 1024, 1024), 1024)

    def value_place(part, place, core):
        rows = pl.ds(pl.multiple_of((place % 2) * 128, 128), 128)
        return abuf.at[part * 2 + place // 2, rows, value_lanes(core)]

    def finish(part, group):
        for h in range(group * 4, group * 4 + 4):
            rows = slice(part * 1024 + h * 128, part * 1024 + (h + 1) * 128)
            head_latent = (acc[rows, :] / ls[rows, :1]).astype(BF16)
            tile = upv[:, :, h * 32 : (h + 1) * 32, :].reshape(LATENT, VDIM)
            value = jnp.dot(head_latent, tile, preferred_element_type=F32).astype(BF16)
            lanes = pl.ds(pl.multiple_of(c * 1024 + h * VDIM, VDIM), VDIM)
            abuf[part * 2 + x // 2, pl.ds(pl.multiple_of((x % 2) * 128, 128), 128), lanes] = value
        rows = pl.ds(pl.multiple_of((x % 2) * 128, 128), 128)
        lanes = pl.ds(pl.multiple_of(c * 1024 + group * 512, 512), 512)
        piece = abuf.at[part * 2 + x // 2, rows, lanes]
        for d in (1, 3, 2):
            send(piece, piece, ra.at[part, d], at(dx=d))
        send(piece, piece, ras.at[part], at(dc=1))

    def values_forward(part):
        for d in (1, 3, 2):
            piece = value_place(part, x_from[d], c)
            arrived(piece, ra.at[part, d])
            send(piece, piece, ras.at[part], at(dc=1))

    def values_ready(part):
        arrived(abuf.at[pl.ds(part * 2, 2), :, value_lanes(1 - c)], ras.at[part])

    def rest_of_chunks(part, group):
        @pl.when(y == 3)
        def _():
            attend([(i, part, group) for i in (1, 2, 3)])

        @pl.when(y < 3)
        def _():
            def step(i, carry):
                attend([(i, part, group)])
                return carry

            lax.fori_loop(1, y + 1, step, 0)

    for d in (1, 3, 2):
        arrived(upk.at[1, y_from[d], x], ru1.at[1, d])
    for d in (1, 3, 2):
        send(upk.at[1, :, x], upk.at[1, :, x], ru2.at[1, d], at(dx=d))
    make_queries(0)
    keys_far(0)
    keys_along_z(2)
    keys_ready(0)
    attend([(0, 0, 0), (0, 1, 0)], True)
    keys_relay(1)
    keys_along_z(3)
    for d in (1, 3, 2):
        arrived(upk.at[1, :, x_from[d]], ru2.at[1, d])
    for d in (1, 3, 2):
        arrived(upv.at[y_from[d], x], rv1.at[d])
    for d in (1, 3, 2):
        send(upv.at[:, x], upv.at[:, x], rv2.at[d], at(dx=d))
    make_queries(1)
    attend([(0, 0, 1), (0, 1, 1)], True)
    keys_far(1)
    keys_relay(2)
    keys_ready(1)
    needed(1, lambda: attend([(1, 0, 0), (1, 0, 1)]))
    keys_far(2)
    keys_relay(3)
    keys_ready(2)
    needed(2, lambda: attend([(2, 0, 0), (2, 0, 1)]))
    weight_relay()
    keys_far(3)
    for d in (1, 3, 2):
        arrived(upv.at[:, x_from[d]], rv2.at[d])
    keys_ready(3)
    needed(3, lambda: attend([(3, 0, 0), (3, 0, 1)]))
    finish(0, 0)
    finish(0, 1)
    rest_of_chunks(1, 0)
    finish(1, 0)
    rest_of_chunks(1, 1)
    finish(1, 1)
    values_forward(0)
    weight_ready()
    values_ready(0)

    near = (z + 1) % 2
    other = z % 2
    is_own = z // 2 == c
    near_up = (2 * c + near + 4 - z) % 4 == 1
    near_half = jnp.where(near_up, 0, 1)
    z_near = jnp.where(near_up, 1, 3)

    def project(slot, t):
        part = lax.dot_general(
            wbuf[slot], abuf[t], (((1,), (1,)), ((), ())), preferred_element_type=F32
        )
        cbuf[slot, t] = part.astype(BF16)

    def far_copy(t, half):
        return pltpu.make_async_remote_copy(
            src_ref=cbuf.at[other, t, pl.ds(half * (COLS // 2), COLS // 2)], dst_ref=land1.at[t],
            send_sem=sc.at[t, half], recv_sem=rl1.at[t],
            device_id=at(dz=1 if half == 0 else 3), device_id_type=MESH,
        )

    def near_copy(t):
        return pltpu.make_async_remote_copy(
            src_ref=cbuf.at[near, t], dst_ref=land0.at[near_half, t],
            send_sem=sl.at[t], recv_sem=rl0.at[near_half, t],
            device_id=at(dz=z_near), device_id_type=MESH,
        )

    first = jnp.where(is_own, near, other)

    def first_step(t, carry):
        project(first, t)

        @pl.when(jnp.logical_not(is_own))
        def _():
            far_copy(t, 0).start()
            far_copy(t, 1).start()

        return carry

    def second_step(t, carry):
        project(1 - first, t)
        return carry

    def near_step(t, carry):
        arrived(land1.at[t], rl1.at[t])
        rows = pl.ds(near_half * (COLS // 2), COLS // 2)
        total = cbuf[near, t, rows].astype(F32) + land1[t].astype(F32)
        cbuf[near, t, rows] = total.astype(BF16)
        near_copy(t).start()
        return carry

    receiver = x // 2

    def final_copy(t, k):
        place = (t % 2) * 2 + k
        lanes = pl.ds(pl.multiple_of((t // 2) * 128, 128), 128)
        source, target = fin.at[t, :, k * 128 : (k + 1) * 128], outbuf.at[x % 2, :, lanes]
        here = jnp.logical_and(place == x, receiver == c)
        local = pltpu.make_async_copy(source, target, rf.at[x % 2])
        remote = pltpu.make_async_remote_copy(
            src_ref=source, dst_ref=target, send_sem=sa.at[t, k], recv_sem=rf.at[x % 2],
            device_id=(y * 4 + place, z * 2 + receiver), device_id_type=MESH,
        )
        return here, local, remote

    def final_step(t, carry):
        arrived(land0.at[0, t], rl0.at[0, t])
        arrived(land0.at[1, t], rl0.at[1, t])
        total = cbuf[other, t].astype(F32) + land0[0, t].astype(F32) + land0[1, t].astype(F32)
        fin[t] = total.astype(BF16)
        for k in range(2):
            here, local, remote = final_copy(t, k)
            pl.when(here)(local.start)
            pl.when(jnp.logical_not(here))(remote.start)
        return carry

    lax.fori_loop(0, 2, first_step, 0)
    lax.fori_loop(0, 2, second_step, 0)
    lax.fori_loop(0, 2, near_step, 0)
    values_forward(1)
    values_ready(1)
    lax.fori_loop(2, 4, first_step, 0)
    lax.fori_loop(2, 4, second_step, 0)

    @pl.when(is_own)
    def _():
        lax.fori_loop(0, 2, final_step, 0)

    lax.fori_loop(2, 4, near_step, 0)

    @pl.when(is_own)
    def _():
        lax.fori_loop(2, 4, final_step, 0)

    for k in range(2):
        arrived(outbuf.at[k], rf.at[k])
    out[:COLS, :] = outbuf[0]
    out[COLS:, :] = outbuf[1]

    for ref, k, condition in pending:
        if condition is None:
            arrived(ref, ssem.at[k])
        else:
            pl.when(condition)(functools.partial(lambda r, n: arrived(r, ssem.at[n]), ref, k))

    @pl.when(jnp.logical_not(own_weight))
    def _():
        sibling_weight.wait_send()

    def sent_near(t, carry):
        near_copy(t).wait_send()
        return carry

    def sent_far(t, carry):
        far_copy(t, 0).wait_send()
        far_copy(t, 1).wait_send()
        return carry

    def sent_final(t, carry):
        for k in range(2):
            here, local, remote = final_copy(t, k)
            pl.when(jnp.logical_not(here))(remote.wait_send)
        return carry

    lax.fori_loop(0, 4, sent_near, 0)

    @pl.when(jnp.logical_not(is_own))
    def _():
        lax.fori_loop(0, 4, sent_far, 0)

    @pl.when(is_own)
    def _():
        lax.fori_loop(0, 4, sent_final, 0)


def body(queries, latent_keys, up_keys, up_values, out_weight, keys_scale, values_scale, out_scale):
    vmem = pl.BlockSpec(memory_space=pltpu.VMEM)
    smem = pl.BlockSpec(memory_space=pltpu.SMEM)
    dma = pltpu.SemaphoreType.DMA
    result = pl.pallas_call(
        kernel,
        out_shape=jax.ShapeDtypeStruct((2 * COLS, TOKENS), BF16),
        in_specs=[vmem] * 5 + [smem] * 3,
        out_specs=vmem,
        scratch_shapes=[
            pltpu.VMEM((4, WIDE, CHUNK), BF16),
            pltpu.VMEM((2, 4, 4, 32, LATENT), BF16),
            pltpu.VMEM((4, 4, 256, VDIM), BF16),
            pltpu.VMEM((HEADS * TOKENS, WIDE), BF16),
            pltpu.VMEM((HEADS * TOKENS, LATENT), F32),
            pltpu.VMEM((HEADS * TOKENS, 128), F32),
            pltpu.VMEM((HEADS * TOKENS, 128), F32),
            pltpu.VMEM((2, COLS, 2048), BF16),
            pltpu.VMEM((COLS, 1024), BF16),
            pltpu.VMEM((4, TOKENS, 2048), BF16),
            pltpu.VMEM((2, 4, COLS, TOKENS), BF16),
            pltpu.VMEM((4, COLS // 2, TOKENS), BF16),
            pltpu.VMEM((2, 4, COLS, TOKENS), BF16),
            pltpu.VMEM((4, COLS, TOKENS), BF16),
            pltpu.VMEM((2, COLS, TOKENS), BF16),
            dma((128,)),
            dma((1,)),
            dma((4, 2)),
            dma((4, 2)),
            dma((4,)),
            dma,
            dma((4,)),
            dma((4, 4)),
            dma((4,)),
            dma((3, 4)),
            dma((3, 4)),
            dma((4,)),
            dma((4,)),
            dma((2, 2)),
            dma((2,)),
            dma((2, 4)),
            dma((2,)),
            dma((4,)),
            dma((2, 4)),
            dma((2,)),
        ],
        compiler_params=pltpu.CompilerParams(
            collective_id=0, has_side_effects=True, vmem_limit_bytes=56 * 2**20
        ),
        name="attention",
    )(
        queries, latent_keys.T, up_keys, up_values, out_weight.swapaxes(1, 2),
        keys_scale.T, values_scale.T, out_scale.T,
    )
    return result.T


def solution(mesh):
    return jax.shard_map(
        body,
        mesh=mesh,
        in_specs=(
            P("ctx", "shard"),
            P("ctx", None),
            P("shard", "ctx", None),
            P("shard", "ctx", None),
            P("shard", None, "ctx"),
            P(),
            P(),
            P(),
        ),
        out_specs=P("ctx", "shard"),
        check_vma=False,
    )
```

time: 130 us -> 95.7 us (0.74)
  Pallas kernels: 121 us -> 93.5 us
  local copies, waits for them, and re-layouts: 8.69 us -> 1.99 us
    pallas_call x1, Pallas kernels: 121 us -> 93.5 us  [body(): pl.pallas_call(kernel, out_shape=jax.ShapeDtypeStruct((2 * COLS, TOKENS),...]
    unnamed x10 -> x0, local copies, waits for them, and re-layouts: 8.69 us -> none
    transpose x0 -> x1, local copies, waits for them, and re-layouts: none -> 1.99 us  [body(): return result.T]
where the time goes in v2:
time: 95.7 us; the launch traced here: 95.5 us
  Pallas kernels  93.5 us (98%)
  local copies, waits for them, and re-layouts  1.99 us (2%)
    pallas_call x1, Pallas kernels, body(): pl.pallas_call(kernel, out_shape=jax.ShapeDtypeStruct((2 * COLS, TOKENS),...  93.5 us
    transpose x1, local copies, waits for them, and re-layouts, body(): return result.T  1.99 us

profile of v2, /device:TPU:30, one launch (start us, length us, event | category | flops | bytes accessed | tf_op | source)
XLA Modules:
  0.0 95.5 jit_solution(10447460255561789034)
XLA Ops:
  0.0 93.5 %attention.1 = bf16[896,256]{1,0:T(8,128)(2,1)} custom-call(bf16[256,1536]{1,0:T(8,128)(2,1)} %queries.1, bf16[576,256]{1,0:T(8,128)(2,1)} %bitcast.8, bf16[8,8,512]{2,1,0:T(8,128)(2,1)} %up_keys.1, bf16[8,32,128]{2,1,0:T(8,128)(2,1)} %up_values.1, bf16[8,448,128]{2,1,0:T(8,128)(2,1)} %bitcast.7, s32[4,64]{1,0:T(4,128)} %bitcast.10, s32[4,64]{1,0:T(4,128)} %bitcast.11, ...), custom_call_target="tpu_custom_call" | custom-call | tf_op jit(solution)/shard_map/attention/pallas_call | solution.py:513
  93.5 2.0 %copy.9 = bf16[256,896]{1,0:T(8,128)(2,1)} copy(bf16[256,896]{0,1:T(8,128)(2,1)} %bitcast.6) | data formatting | bytes 917504 | tf_op jit(solution)/shard_map/transpose | solution.py:563

commit v3 on v2

--- a/solution.py
+++ b/solution.py
@@ -302,15 +302,23 @@
         rows = pl.ds(pl.multiple_of((x % 2) * 128, 128), 128)
         lanes = pl.ds(pl.multiple_of(c * 1024 + group * 512, 512), 512)
         piece = abuf.at[part * 2 + x // 2, rows, lanes]
-        for d in (1, 3, 2):
+        for d in (1, 3):
             send(piece, piece, ra.at[part, d], at(dx=d))
         send(piece, piece, ras.at[part], at(dc=1))
 
-    def values_forward(part):
-        for d in (1, 3, 2):
+    def values_relay(part):
+        for d in (1, 3):
             piece = value_place(part, x_from[d], c)
             arrived(piece, ra.at[part, d])
+            start = pl.multiple_of((x_from[d] % 2) * 128 + (d // 2) * 64, 64)
+            half = abuf.at[part * 2 + x_from[d] // 2, pl.ds(start, 64), value_lanes(c)]
+            send(half, half, ra.at[part, 2], at(dx=d))
             send(piece, piece, ras.at[part], at(dc=1))
+
+    def values_far(part):
+        piece = value_place(part, x_from[2], c)
+        arrived(piece, ra.at[part, 2])
+        send(piece, piece, ras.at[part], at(dc=1))
 
     def values_ready(part):
         arrived(abuf.at[pl.ds(part * 2, 2), :, value_lanes(1 - c)], ras.at[part])
@@ -332,13 +340,13 @@
         arrived(upk.at[1, y_from[d], x], ru1.at[1, d])
     for d in (1, 3, 2):
         send(upk.at[1, :, x], upk.at[1, :, x], ru2.at[1, d], at(dx=d))
-    make_queries(0)
     keys_far(0)
     keys_along_z(2)
+    keys_along_z(3)
+    make_queries(0)
     keys_ready(0)
     attend([(0, 0, 0), (0, 1, 0)], True)
     keys_relay(1)
-    keys_along_z(3)
     for d in (1, 3, 2):
         arrived(upk.at[1, :, x_from[d]], ru2.at[1, d])
     for d in (1, 3, 2):
@@ -349,25 +357,26 @@
     attend([(0, 0, 1), (0, 1, 1)], True)
     keys_far(1)
     keys_relay(2)
+    keys_relay(3)
     keys_ready(1)
     needed(1, lambda: attend([(1, 0, 0), (1, 0, 1)]))
     keys_far(2)
-    keys_relay(3)
+    keys_far(3)
     keys_ready(2)
     needed(2, lambda: attend([(2, 0, 0), (2, 0, 1)]))
     weight_relay()
-    keys_far(3)
-    for d in (1, 3, 2):
-        arrived(upv.at[:, x_from[d]], rv2.at[d])
     keys_ready(3)
     needed(3, lambda: attend([(3, 0, 0), (3, 0, 1)]))
+    for d in (1, 3, 2):
+        arrived(upv.at[:, x_from[d]], rv2.at[d])
     finish(0, 0)
     finish(0, 1)
     rest_of_chunks(1, 0)
     finish(1, 0)
     rest_of_chunks(1, 1)
+    values_relay(0)
     finish(1, 1)
-    values_forward(0)
+    values_far(0)
     weight_ready()
     values_ready(0)
 
@@ -449,8 +458,9 @@
 
     lax.fori_loop(0, 2, first_step, 0)
     lax.fori_loop(0, 2, second_step, 0)
+    values_relay(1)
     lax.fori_loop(0, 2, near_step, 0)
-    values_forward(1)
+    values_far(1)
     values_ready(1)
     lax.fori_loop(2, 4, first_step, 0)
     lax.fori_loop(2, 4, second_step, 0)

time: 95.7 us -> 93.2 us (0.974)
  Pallas kernels: 93.5 us -> 91.1 us
    pallas_call x1, Pallas kernels: 93.5 us -> 91.1 us  [body(): pl.pallas_call(kernel, out_shape=jax.ShapeDtypeStruct((2 * COLS, TOKENS),...]
where the time goes in v3:
time: 93.2 us; the launch traced here: 93.1 us
  Pallas kernels  91.1 us (98%)
  local copies, waits for them, and re-layouts  1.99 us (2%)
    pallas_call x1, Pallas kernels, body(): pl.pallas_call(kernel, out_shape=jax.ShapeDtypeStruct((2 * COLS, TOKENS),...  91.1 us
    transpose x1, local copies, waits for them, and re-layouts, body(): return result.T  1.99 us

profile of v3, /device:TPU:30, one launch (start us, length us, event | category | flops | bytes accessed | tf_op | source)
XLA Modules:
  0.0 93.1 jit_solution(10429226946012523378)
XLA Ops:
  0.0 91.1 %attention.1 = bf16[896,256]{1,0:T(8,128)(2,1)} custom-call(bf16[256,1536]{1,0:T(8,128)(2,1)} %queries.1, bf16[576,256]{1,0:T(8,128)(2,1)} %bitcast.8, bf16[8,8,512]{2,1,0:T(8,128)(2,1)} %up_keys.1, bf16[8,32,128]{2,1,0:T(8,128)(2,1)} %up_values.1, bf16[8,448,128]{2,1,0:T(8,128)(2,1)} %bitcast.7, s32[4,64]{1,0:T(4,128)} %bitcast.10, s32[4,64]{1,0:T(4,128)} %bitcast.11, ...), custom_call_target="tpu_custom_call" | custom-call | tf_op jit(solution)/shard_map/attention/pallas_call | solution.py:523
  91.1 2.0 %copy.9 = bf16[256,896]{1,0:T(8,128)(2,1)} copy(bf16[256,896]{0,1:T(8,128)(2,1)} %bitcast.6) | data formatting | bytes 917504 | tf_op jit(solution)/shard_map/transpose | solution.py:573

commit v4 on v3

--- a/solution.py
+++ b/solution.py
@@ -25,7 +25,7 @@
 
 PEERS = (
     [(0, d, 0, k) for d in (1, 2, 3) for k in (0, 1)]
-    + [(d, 0, 0, k) for d in (1, 2, 3) for k in (0, 1)]
+    + [(1, 0, 0, 0), (2, 0, 0, 0), (3, 0, 0, 0), (1, 0, 0, 1), (3, 0, 0, 1)]
     + [(0, 0, d, 0) for d in (1, 2, 3)]
     + [(0, 0, 0, 1)]
 )
@@ -459,8 +459,8 @@
     lax.fori_loop(0, 2, first_step, 0)
     lax.fori_loop(0, 2, second_step, 0)
     values_relay(1)
+    values_far(1)
     lax.fori_loop(0, 2, near_step, 0)
-    values_far(1)
     values_ready(1)
     lax.fori_loop(2, 4, first_step, 0)
     lax.fori_loop(2, 4, second_step, 0)

time: 93.2 us -> 97.1 us (1.042)
  Pallas kernels: 91.1 us -> 94.9 us
    pallas_call x1, Pallas kernels: 91.1 us -> 94.9 us  [body(): pl.pallas_call(kernel, out_shape=jax.ShapeDtypeStruct((2 * COLS, TOKENS),...]
where the time goes in v4:
time: 97.1 us; the launch traced here: 96.9 us
  Pallas kernels  94.9 us (98%)
  local copies, waits for them, and re-layouts  1.99 us (2%)
    pallas_call x1, Pallas kernels, body(): pl.pallas_call(kernel, out_shape=jax.ShapeDtypeStruct((2 * COLS, TOKENS),...  94.9 us
    transpose x1, local copies, waits for them, and re-layouts, body(): return result.T  1.99 us

profile of v4, /device:TPU:30, one launch (start us, length us, event | category | flops | bytes accessed | tf_op | source)
XLA Modules:
  0.0 96.9 jit_solution(6412908826198138049)
XLA Ops:
  0.0 94.9 %attention.1 = bf16[896,256]{1,0:T(8,128)(2,1)} custom-call(bf16[256,1536]{1,0:T(8,128)(2,1)} %queries.1, bf16[576,256]{1,0:T(8,128)(2,1)} %bitcast.8, bf16[8,8,512]{2,1,0:T(8,128)(2,1)} %up_keys.1, bf16[8,32,128]{2,1,0:T(8,128)(2,1)} %up_values.1, bf16[8,448,128]{2,1,0:T(8,128)(2,1)} %bitcast.7, s32[4,64]{1,0:T(4,128)} %bitcast.10, s32[4,64]{1,0:T(4,128)} %bitcast.11, ...), custom_call_target="tpu_custom_call" | custom-call | tf_op jit(solution)/shard_map/attention/pallas_call | solution.py:523
  94.9 2.0 %copy.9 = bf16[256,896]{1,0:T(8,128)(2,1)} copy(bf16[256,896]{0,1:T(8,128)(2,1)} %bitcast.6) | data formatting | bytes 917504 | tf_op jit(solution)/shard_map/transpose | solution.py:573
